TPU v7x, 128 devices: a whole 4x4x4 slice. The times are simulated.
128 devices in a mesh: dp: 16 (over x_hi, y, core), frame: 8 (over z, x_lo).
Axes of the slice: x: 4 (x_hi: 2, x_lo: 2; x = x_hi * 2 + x_lo), y: 4, z: 4, core: 2. Of those that a mesh axis runs over, the one named last changes fastest.
Arguments:
- clips_in: bfloat16 [16, 8, 8, 96, 640], P('dp', 'frame'), may hold values from -40 to 40
- teacher: bfloat16 [16, 8, 8, 96, 640], P('dp', 'frame'), may hold values from -6 to 6
- spatial_weight: bfloat16 [3, 3, 640, 640], replicated, may hold values from -0.078125 to 0.078125
- temporal_weight: bfloat16 [3, 640, 640], replicated, may hold values from -0.125 to 0.125
- norm_gain: float32 [640], replicated, may hold values from 0.5 to 1.5
- norm_bias: float32 [640], replicated, may hold values from -3 to 3
Outputs:
- spatial_grad: float32 [5760, 640], P(('dp', 'frame'))
- temporal_grad: float32 [1920, 640], P(('dp', 'frame'))
- gain_grad: float32 [640], replicated
- bias_grad: float32 [640], replicated
- loss: float32 [], replicated
All inputs are finite; a program needn't handle non-finite values.
Results may differ from a plain program's by a relative error of at most 0.0045.
Values may be sent and summed in bfloat16 or wider, within the bound.
A program may use at most 128 MiB of HBM per device.

v0:
```python
import jax
import jax.numpy as jnp
from jax import lax
from jax.experimental import pallas as pl
from jax.experimental.pallas import tpu as pltpu
from jax.sharding import PartitionSpec as P

GROUPS = 32
EPSILON = 1e-05
F32 = jnp.float32
BF16 = jnp.bfloat16
MESH = pl.DeviceIdType.MESH

FRAMES = 8
ROWS = 8
COLS = 96
C = 640
OWN = COLS // FRAMES
WIDE = OWN + 2
CELLS = OWN * FRAMES * ROWS
CELLS_WIDE = WIDE * FRAMES * ROWS
SLAB = FRAMES * ROWS
BLOCK = 16
TILES = C // 128
AXES = ((2, 0, 1), (1, 2, 0), (0, 1, 2), (0, 1, 2), (1, 2, 0), (2, 0, 1))
LANES = ((0, C), (0, C), (0, C), (0, 256), (256, 512), (512, C))
UNITS = 6


def rem(a, b):
    return lax.rem(a, jnp.int32(b))


def div(a, b):
    return lax.div(a, jnp.int32(b))


class Place:
    def __init__(self):
        self.dp = lax.axis_index("dp")
        self.fr = lax.axis_index("frame")
        self.core = rem(self.dp, 2)
        self.y = rem(div(self.dp, 2), 4)
        self.xh = div(self.dp, 8)
        self.z = div(self.fr, 2)
        self.xl = rem(self.fr, 2)
        self.x = 2 * self.xh + self.xl
        self.group = self.xh * 4 + self.y
        self.along = (self.x, self.y, self.z)

        self.at = [[rem(v + step, 4) for step in range(4)] for v in self.along]
        self.dp_x = [div(v, 2) * 8 for v in self.at[0]]
        self.fr_x = [rem(v, 2) for v in self.at[0]]
        self.dp_y = [2 * v for v in self.at[1]]
        self.fr_z = [2 * v for v in self.at[2]]

    def further(self, *steps):
        x, y, z = steps
        return (self.dp_x[x] + self.dp_y[y] + self.core, self.fr_z[z] + self.fr_x[x])

    def along_axis(self, axis, step):
        return self.further(*(step if axis == n else 0 for n in range(3)))

    def in_plane(self, one, step_one, two, step_two):
        return self.further(
            *(step_one if n == one else step_two if n == two else 0 for n in range(3))
        )


def kernel(
    x_hbm, t_hbm, gain_ref, bias_ref, w_hbm, wt_hbm,
    rows_out, small_out,
    w, wt, xraw, traw, xs, ts, xr, tr, stats, hid, hid_t, hid_p, s3, s3_t, s3_p, go, gs, xj, acc,
    stage0, stage1, stage2, stage3, stage4, stage5,
    r10, r11, r12, r13, r14, r15,
    p20, p21, p22, p23, p24, p25,
    r20, r21, r22, r23, r24, r25,
    small_a, small_b,
    w_sem, own_sem, x_send, x_recv, t_send, t_recv, st_send, st_recv, pair_send, pair_recv,
    hp_send, hp_recv, r1_send, r1_recv, r2_send, r2_recv, a_send, a_recv, b_send, b_recv,
):
    me = Place()
    dp, fr, core = me.dp, me.fr, me.core
    gs3 = s3
    g3 = hid
    stage = (stage0, stage1, stage2, stage3, stage4, stage5)
    r1 = (r10, r11, r12, r13, r14, r15)
    p2 = (p20, p21, p22, p23, p24, p25)
    r2 = (r20, r21, r22, r23, r24, r25)

    def get(at):
        return jnp.concatenate([acc[l, at, :] for l in range(TILES)], axis=1)

    def put(at, value):
        for l in range(TILES):
            acc[l, at, :] = value[:, l * 128 : (l + 1) * 128]

    load_x = pltpu.make_async_copy(x_hbm, xraw, own_sem.at[0])
    load_x.start()
    load_t = pltpu.make_async_copy(t_hbm, traw, own_sem.at[1])
    load_t.start()

    w_copies = []
    for a in range(3):
        for c in range(3):
            w_copies.append(
                pltpu.make_async_copy(
                    w_hbm.at[a, c], w.at[c, pl.ds(a * C, C)], w_sem.at[3 * a + c]
                )
            )
    w_copies.append(pltpu.make_async_copy(wt_hbm, wt, w_sem.at[9]))
    for copy in w_copies:
        copy.start()

    barrier = pltpu.get_barrier_semaphore()

    def greet(device):
        pl.semaphore_signal(barrier, inc=1, device_id=device, device_id_type=MESH)

    for axis in range(3):
        for s in range(1, 4):
            greet(me.along_axis(axis, s))
    for one, two in ((0, 1), (1, 2), (0, 2)):
        for s in range(1, 4):
            for t in range(1, 4):
                greet(me.in_plane(one, s, two, t))
    across = 1 - 2 * core
    for s in range(4):
        greet((me.dp_x[0] + me.dp_y[s] + core + across, fr))
    partner = (dp + across, fr)

    load_x.wait()

    def moment_body(i, carry):
        total, square = carry
        v = xraw[i].astype(F32)
        put(pl.ds(pl.multiple_of(i * COLS, 8), COLS), v)
        v = v.reshape(COLS // 8, 8, C)
        return (total + jnp.sum(v, axis=0), square + jnp.sum(v * v, axis=0))

    zero = jnp.zeros((8, C), F32)
    total, square = lax.fori_loop(0, ROWS, moment_body, (zero, zero))
    stats[fr, 0:8] = total
    stats[fr, 8:16] = square

    pl.semaphore_wait(barrier, 40)

    sends = []
    for s in range(1, 8):
        to = rem(fr + s, 8)
        copy = pltpu.make_async_remote_copy(
            stats.at[fr], stats.at[fr], st_send.at[s], st_recv.at[s],
            device_id=(dp, to), device_id_type=MESH,
        )
        copy.start()
        sends.append(copy)

    def two_columns(first, second):
        return jnp.concatenate(
            [
                jnp.concatenate(
                    [acc[l, pl.ds(j, ROWS, stride=COLS), :] for l in range(TILES)], axis=1
                )
                for j in (first, second)
            ],
            axis=0,
        ).astype(BF16)

    def x_share(ref, to):
        def body(jj, carry):
            j = OWN * to - 1 + 2 * jj
            ref[pl.ds(pl.multiple_of(16 * jj, 16), 16), :] = two_columns(
                jnp.maximum(j, 0), jnp.minimum(j + 1, COLS - 1)
            )
            return carry

        lax.fori_loop(0, WIDE // 2, body, 0)

    def t_share(ref, to):
        def body(jj, carry):
            j = OWN * to + 2 * jj
            ref[pl.ds(pl.multiple_of(16 * jj, 16), 16), :] = two_columns(j, j + 1)
            return carry

        lax.fori_loop(0, OWN // 2, body, 0)

    for s in range(1, 8):
        to = rem(fr + s, 8)
        x_share(xs.at[s], to)
        copy = pltpu.make_async_remote_copy(
            xs.at[s], xr.at[fr], x_send.at[s], x_recv.at[s],
            device_id=(dp, to), device_id_type=MESH,
        )
        copy.start()
        sends.append(copy)
    x_share(xr.at[fr], fr)

    load_t.wait()

    def teacher_body(i, carry):
        put(pl.ds(pl.multiple_of(i * COLS, 8), COLS), traw[i].astype(F32))
        return carry

    lax.fori_loop(0, ROWS, teacher_body, 0)
    for s in range(1, 8):
        to = rem(fr + s, 8)
        t_share(ts.at[s], to)
    t_share(tr.at[fr], fr)

    hid_t[9 * C :, :] = jnp.zeros((48, CELLS), BF16)
    s3_t[3 * C :, :] = jnp.zeros((16, CELLS), BF16)

    row = lax.broadcasted_iota(jnp.int32, (C, C), 0)
    col = lax.broadcasted_iota(jnp.int32, (C, C), 1)
    same = (
        lax.shift_right_logical(row * 3277, 16) == lax.shift_right_logical(col * 3277, 16)
    ).astype(F32).astype(BF16)
    for s in range(1, 8):
        sender = rem(fr - s + 8, 8)
        pltpu.make_async_remote_copy(
            stats.at[sender], stats.at[sender], st_send.at[s], st_recv.at[s],
            device_id=(dp, sender), device_id_type=MESH,
        ).wait_recv()
    moments = stats[0]
    for f in range(1, FRAMES):
        moments = moments + stats[f]
    high = moments.astype(BF16)
    rest = moments - high.astype(F32)
    middle = rest.astype(BF16)
    low = (rest - middle.astype(F32)).astype(BF16)
    wide = (
        jnp.dot(high, same, preferred_element_type=F32)
        + jnp.dot(middle, same, preferred_element_type=F32)
        + jnp.dot(low, same, preferred_element_type=F32)
    )
    size = float(FRAMES * ROWS * COLS * (C // GROUPS))
    mean = jnp.sum(wide[0:8], axis=0, keepdims=True) / size
    variance = jnp.sum(wide[8:16], axis=0, keepdims=True) / size - mean * mean
    inverse = lax.rsqrt(variance + EPSILON)
    gain = gain_ref[...].reshape(1, C)
    bias = bias_ref[...].reshape(1, C)

    for s in range(1, 8):
        sender = rem(fr - s + 8, 8)
        pltpu.make_async_remote_copy(
            xr.at[sender], xr.at[sender], x_send.at[s], x_recv.at[s],
            device_id=(dp, sender), device_id_type=MESH,
        ).wait_recv()
        copy = pltpu.make_async_remote_copy(
            ts.at[s], tr.at[fr], t_send.at[s], t_recv.at[s],
            device_id=(dp, rem(fr + s, 8)), device_id_type=MESH,
        )
        copy.start()
        sends.append(copy)

    cell_row = rem(lax.broadcasted_iota(jnp.int32, (BLOCK, C), 0), 8)

    def valid_of(j):
        outside = ((j == 0) & (fr == 0)) | ((j == WIDE - 1) & (fr == FRAMES - 1))
        return 1.0 - outside.astype(F32)

    def sigmoid(v):
        return 0.5 * jnp.tanh(0.5 * v) + 0.5

    def store_row_shifts(ref, at, value, first, last):
        ref[at, first * C : (first + 1) * C] = jnp.where(
            cell_row == 0, 0.0, pltpu.roll(value, 1, 0)
        ).astype(BF16)
        ref[at, C : 2 * C] = value.astype(BF16)
        ref[at, last * C : (last + 1) * C] = jnp.where(
            cell_row == 7, 0.0, pltpu.roll(value, BLOCK - 1, 0)
        ).astype(BF16)

    def hidden_body(n, carry):
        p = div(n, WIDE // 2)
        jj = rem(n, WIDE // 2)
        at = pl.ds(pl.multiple_of(jj * 16, 16), 16)
        even = xr[2 * p, at].astype(F32)
        odd = xr[2 * p + 1, at].astype(F32)
        for h in range(2):
            j = 2 * jj + h
            v = jnp.concatenate([even[8 * h : 8 * h + 8], odd[8 * h : 8 * h + 8]], axis=0)
            normed = (v - mean) * inverse * gain + bias
            value = normed * sigmoid(normed) * valid_of(j)
            dst = pl.ds(pl.multiple_of(j * SLAB + p * 16, 16), 16)
            xj[dst, :] = v.astype(BF16)
            store_row_shifts(hid, dst, value, 0, 2)
        return carry

    lax.fori_loop(0, 4 * (WIDE // 2), hidden_body, 0)

    def pair_copy(src, dst, n):
        return pltpu.make_async_remote_copy(
            src, dst, pair_send.at[n], pair_recv.at[n], device_id=partner, device_id_type=MESH
        )

    pad8 = jnp.zeros((8, C), F32)

    def store_frame_shifts(ref, at, value, before, after):
        ref[at, before * C : (before + 1) * C] = jnp.concatenate(
            [pad8, value[: SLAB - 8]], axis=0
        ).astype(BF16)
        ref[at, C : 2 * C] = value.astype(BF16)
        ref[at, after * C : (after + 1) * C] = jnp.concatenate(
            [value[8:], pad8], axis=0
        ).astype(BF16)

    def rows_of(b):
        return pl.ds(pl.multiple_of(b * 256, 256), 256)

    def hidden_pair(m, lanes=pl.ds(0, CELLS)):
        src = pl.ds(pl.multiple_of(720 * m + 352 * (1 - core), 16), 384)
        return pltpu.make_async_remote_copy(
            hid_t.at[src, lanes], hid_p.at[m, :, lanes], hp_send.at[m], hp_recv.at[m],
            device_id=partner, device_id_type=MESH,
        )

    for copy in w_copies:
        copy.wait()

    def forward_body(b, carry):
        windows = [
            hid[pl.ds(pl.multiple_of(b * 256 + c * SLAB, 64), 256), :] for c in range(3)
        ]
        total = jnp.dot(
            jnp.concatenate(windows, axis=1), w[...].reshape(9 * C, C),
            preferred_element_type=F32,
        )
        for c in range(3):
            for a in range(3):
                top = (a * 3 + c) * C
                for half in range(2):
                    src = pl.ds(pl.multiple_of(b * 256 + c * SLAB + half * 128, 64), 128)
                    dst = pl.ds(pl.multiple_of(b * 256 + half * 128, 128), 128)
                    hid_t[top : top + C, dst] = hid[src, a * C : (a + 1) * C].T

        def hidden_send(n, carry):
            hidden_pair(rem(me.group + 1 + n, 8), rows_of(b)).start()
            return carry

        lax.fori_loop(0, 8, hidden_send, 0)
        for k in range(4):
            at = pl.ds(pl.multiple_of(b * 256 + k * SLAB, SLAB), SLAB)
            store_frame_shifts(s3, at, total[k * SLAB : (k + 1) * SLAB], 0, 2)
        put(rows_of(b), jnp.dot(s3[rows_of(b), :], wt[...], preferred_element_type=F32))
        for t in range(3):
            for half in range(2):
                at = pl.ds(pl.multiple_of(b * 256 + half * 128, 128), 128)
                s3_t[t * C : (t + 1) * C, at] = s3[at, t * C : (t + 1) * C].T
        for m in range(8):
            src = pl.ds(pl.multiple_of(240 * m + 112 * (1 - core), 16), 144)
            pair_copy(s3_t.at[src, rows_of(b)], s3_p.at[m, :, rows_of(b)], 2).start()
        return carry

    lax.fori_loop(0, 3, forward_body, 0)

    for s in range(1, 8):
        sender = rem(fr - s + 8, 8)
        pltpu.make_async_remote_copy(
            tr.at[sender], tr.at[sender], t_send.at[s], t_recv.at[s],
            device_id=(dp, sender), device_id_type=MESH,
        ).wait_recv()

    scale = float(16 * FRAMES * ROWS * COLS) ** (-0.5)

    def nt(lhs, rhs):
        return lax.dot_general(lhs, rhs, (((1,), (1,)), ((), ())), preferred_element_type=F32)

    def backward_body(b, loss):
        for half in range(2):
            jj = 2 * b + half
            at = pl.ds(pl.multiple_of(jj * 16, 16), 16)
            target = [tr[f, at].astype(F32) for f in range(FRAMES)]
            for h in range(2):
                j = 2 * jj + h
                own = pl.ds(pl.multiple_of(j * SLAB, SLAB), SLAB)
                wide_at = pl.ds(pl.multiple_of((j + 1) * SLAB, SLAB), SLAB)
                taught = jnp.concatenate([t[8 * h : 8 * h + 8] for t in target], axis=0)
                out = get(own).astype(BF16).astype(F32)
                error = xj[wide_at, :].astype(F32) + out - taught
                grad = error * scale
                go[0, own, :] = grad.astype(BF16)
                store_frame_shifts(g3, own, grad, 2, 0)
                loss = loss + jnp.sum((error * error).reshape(FRAMES, 8, C), axis=0)
        src = rows_of(b)
        pair_copy(go.at[0, src], go.at[1, src], 1).start()
        total = None
        for t in range(3):
            part = nt(g3[src, t * C : (t + 1) * C], wt[t * C : (t + 1) * C, :])
            total = part if total is None else total + part
        for k in range(16):
            at = pl.ds(pl.multiple_of(b * 256 + 16 * k, 16), 16)
            value = total[16 * k : 16 * k + 16]
            gs[0, at, :] = value.astype(BF16)
            store_row_shifts(gs3, at, value, 2, 0)
        pair_copy(gs.at[0, src], gs.at[1, src], 3).start()
        return loss

    loss = lax.fori_loop(0, 3, backward_body, jnp.zeros((8, C), F32))

    def wait_pair(dst, n):
        pair_copy(dst, dst, n).wait_recv()

    wait_pair(go.at[1], 1)
    wait_pair(s3_p, 2)

    def time_body(n, carry):
        own = jnp.concatenate(
            [
                s3_t[pl.ds(pl.multiple_of(240 * (4 * n + k) + 112 * core, 16), 144), :]
                for k in range(4)
            ],
            axis=0,
        )
        other = s3_p[pl.ds(4 * n, 4)].reshape(576, CELLS)
        both = jnp.concatenate([own, other], axis=1)
        out = jnp.dot(both, go[...].reshape(2 * CELLS, C), preferred_element_type=F32)
        put(pl.ds(0, 576), out)
        for k in range(4):
            for q in range(8):
                cut = 15 * q % 8
                at = pl.ds(pl.multiple_of(144 * k + 15 * q - cut + 8 * core, 8), 24)
                rows = get(at)[cut : cut + 16].astype(BF16)
                zz, xl = q // 2, q % 2
                stage[3][4 * n + k, xl * 4 + zz] = rows[:, 0:256]
                stage[4][4 * n + k, q] = rows[:, 256:512]
                stage[5][4 * n + k, q] = rows[:, 512:C]
        return carry

    lax.fori_loop(0, 2, time_body, 0)

    def first_send(u, src, step, dst, device):
        pltpu.make_async_remote_copy(
            src, dst, r1_send.at[u, step - 1], r1_recv.at[u, step - 1],
            device_id=device, device_id_type=MESH,
        ).start()

    def send_y(u, m):
        mx, my = div(m, 4), rem(m, 4)
        step = rem(my - me.y + 4, 4)

        @pl.when(step != 0)
        def _():
            first_send(
                u, stage[u].at[m], step,
                r1[u].at[step - 1, pl.ds(mx * 8, 8)],
                (me.dp_x[0] + 2 * my + core, fr),
            )

    def send_z(u, m):
        for s in range(1, 4):
            first_send(
                u, stage[u].at[m, pl.ds(me.fr_z[s], 2)], s,
                r1[u].at[s - 1, pl.ds(m * 2, 2)], me.along_axis(2, s),
            )

    def send_x(u, m):
        mx, my = div(m, 4), rem(m, 4)
        for xl in range(2):
            there = 2 * mx + xl
            step = rem(there - me.x + 4, 4)

            @pl.when(step != 0)
            def _():
                first_send(
                    u, stage[u].at[m, pl.ds(xl * 4, 4)], step,
                    r1[u].at[step - 1, pl.ds(my * 4, 4)],
                    (mx * 8 + me.dp_y[0] + core, me.fr_z[0] + xl),
                )

    def time_send(n, carry):
        m = rem(me.group + 1 + n, 8)
        send_x(3, m)
        send_y(4, m)
        send_z(5, m)
        return carry

    lax.fori_loop(0, 8, time_send, 0)

    wait_pair(gs.at[1], 3)

    def space_group(n):
        return rem(me.group + 1 + n, 8)

    def space_cut(n):
        m = space_group(n)
        half = rem(n, 2) * 384 + 8 * core
        for q in range(8):
            cut = 45 * q % 8
            at = pl.ds(pl.multiple_of(half + 45 * q - cut, 8), 56)
            rows = get(at)[cut : cut + 48].astype(BF16)
            zz, xl = q // 2, q % 2
            stage[0][m, q] = rows[0:16]
            stage[1][m, q] = rows[16:32]
            stage[2][m, xl * 4 + zz] = rows[32:48]

    def space_send(n):
        m = space_group(n)
        send_z(0, m)
        send_y(1, m)
        send_x(2, m)

    def space_dot(n):
        m = space_group(n)
        own = hid_t[pl.ds(pl.multiple_of(720 * m + 352 * core, 16), 384), :]
        both = jnp.concatenate([own, hid_p[m]], axis=1)
        out = jnp.dot(both, gs[...].reshape(2 * CELLS, C), preferred_element_type=F32)
        put(pl.ds(pl.multiple_of(rem(n, 2) * 384, 128), 384), out)

    hidden_pair(space_group(0)).wait_recv()
    space_dot(0)

    def space_body(n, carry):
        hidden_pair(space_group(n)).wait_recv()
        space_cut(n - 1)
        space_dot(n)
        space_send(n - 1)
        return carry

    lax.fori_loop(1, 8, space_body, 0)
    space_cut(7)
    space_send(7)

    put(pl.ds(CELLS, 2 * SLAB), jnp.zeros((2 * SLAB, C), F32))

    def grad_hidden(c):
        def body(b, carry):
            src = pl.ds(pl.multiple_of(b * 256, 256), 256)
            dst = pl.ds(pl.multiple_of(b * 256 + c * SLAB, 64), 256)
            total = get(dst) if c > 0 else None
            for a in range(3):
                part = nt(gs3[src, a * C : (a + 1) * C], w[c, a * C : (a + 1) * C, :])
                total = part if total is None else total + part
            put(dst, total)
            return carry

        lax.fori_loop(0, 3, body, 0)

    def first_steps(u, wait):
        for s in range(1, 4):
            copy = pltpu.make_async_remote_copy(
                r1[u].at[s - 1], r1[u].at[s - 1], r1_send.at[u, s - 1], r1_recv.at[u, s - 1],
                device_id=me.along_axis(0, 1), device_id_type=MESH,
            )
            if wait == "recv":
                copy.wait_recv()
            else:
                copy.wait_send()

    def plane_copy(u, src, dst, device):
        return pltpu.make_async_remote_copy(
            src, dst, r2_send.at[u], r2_recv.at[u], device_id=device, device_id_type=MESH
        )

    def plane_all(u):
        return plane_copy(u, r2[u], r2[u], me.along_axis(0, 1))

    def second_phase(u):
        first_steps(u, "recv")
        axis, one, two = AXES[u]
        for step_one in range(4):
            for step_two in range(4):
                n = step_one * 4 + step_two
                if axis == 2:
                    x_half, xl, y = div(me.dp_x[step_one], 8), me.fr_x[step_one], me.at[1][step_two]
                    k = x_half * 8 + y * 2 + xl
                    own = stage[u][x_half * 4 + y, me.fr_z[0] + xl]
                elif axis == 0:
                    y, z = me.at[1][step_one], me.at[2][step_two]
                    k = y * 4 + z
                    own = stage[u][me.xh * 4 + y, me.xl * 4 + z]
                else:
                    q = me.fr_z[step_one] + me.fr_x[step_two]
                    k = me.dp_x[step_two] + q
                    own = stage[u][div(me.dp_x[step_two], 2) + me.y, q]
                total = own.astype(F32)
                for s in range(3):
                    total = total + r1[u][s, k].astype(F32)
                p2[u][n] = total.astype(BF16)
                if n > 0:
                    plane_copy(
                        u, p2[u].at[n], r2[u].at[n - 1],
                        me.in_plane(one, step_one, two, step_two),
                    ).start()

    def last_phase(u):
        plane_all(u).wait_recv()
        total = p2[u][0].astype(F32)
        for n in range(15):
            total = total + r2[u][n].astype(F32)
        low, high = LANES[u]
        top = min(u, 3) * BLOCK
        rows_out[top : top + BLOCK, low:high] = total

    grad_hidden(0)
    for u in range(3, 6):
        second_phase(u)
    grad_hidden(1)
    grad_hidden(2)

    def norm_body(n, carry):
        gain_sum, bias_sum = carry
        at = pl.ds(pl.multiple_of(n * 16, 16), 16)
        centred = (xj[at, :].astype(F32) - mean) * inverse
        normed = centred * gain + bias
        s = sigmoid(normed)
        grad = get(at) * s * (1.0 + normed * (1.0 - s)) * valid_of(div(n, 4))
        weighted = grad * centred
        return (gain_sum + weighted[0:8] + weighted[8:16], bias_sum + grad[0:8] + grad[8:16])

    gain_sum, bias_sum = lax.fori_loop(0, CELLS_WIDE // 16, norm_body, (zero, zero), unroll=2)
    at_plane = me.x * 4 + me.z
    small_a[at_plane, 0:1] = jnp.sum(gain_sum, axis=0, keepdims=True)
    small_a[at_plane, 1:2] = jnp.sum(bias_sum, axis=0, keepdims=True)
    small_a[at_plane, 2:3] = jnp.sum(loss, axis=0, keepdims=True)
    small_a[at_plane, 3:8] = jnp.zeros((5, C), F32)

    for n in range(1, 16):
        pltpu.make_async_remote_copy(
            small_a.at[at_plane], small_a.at[at_plane], a_send, a_recv,
            device_id=me.in_plane(0, n // 4, 2, n % 4), device_id_type=MESH,
        ).start()

    for u in range(3):
        second_phase(u)

    small_all = pltpu.make_async_remote_copy(
        small_a.at[pl.ds(0, 15)], small_a.at[pl.ds(0, 15)], a_send, a_recv,
        device_id=partner, device_id_type=MESH,
    )
    small_all.wait_recv()
    total = small_a[0]
    for f in range(1, 16):
        total = total + small_a[f]
    at_rest = me.y * 2 + core
    small_b[at_rest] = total
    for s in range(4):
        for t in range(2):
            if s + t > 0:
                to = (me.dp_x[0] + me.dp_y[s] + core + t * across, fr)
                pltpu.make_async_remote_copy(
                    small_b.at[at_rest], small_b.at[at_rest], b_send, b_recv,
                    device_id=to, device_id_type=MESH,
                ).start()

    for u in range(3, 6):
        last_phase(u)

    rest_all = pltpu.make_async_remote_copy(
        small_b.at[pl.ds(0, 7)], small_b.at[pl.ds(0, 7)], b_send, b_recv,
        device_id=partner, device_id_type=MESH,
    )
    rest_all.wait_recv()
    total = small_b[0]
    for d in range(1, 8):
        total = total + small_b[d]
    small_out[...] = total

    for u in range(3):
        last_phase(u)

    for copy in sends:
        copy.wait_send()
    small_all.wait_send()
    rest_all.wait_send()
    for m in range(8):
        hidden_pair(m).wait_send()
    pair_copy(go.at[0], go.at[1], 1).wait_send()
    pair_copy(s3_p, s3_p, 2).wait_send()
    pair_copy(gs.at[0], gs.at[1], 3).wait_send()
    for u in range(UNITS):
        first_steps(u, "send")
        plane_all(u).wait_send()


def finish(rows, small, space, time, gain, bias, loss):
    space[...] = rows[0:45]
    time[...] = rows[48:63]
    gain[...] = small[0]
    bias[...] = small[1]
    loss[0, 0] = jnp.sum(small[2:3]) / float(16 * FRAMES * ROWS * COLS * C)


def shards(clips_in, teacher, spatial_weight, temporal_weight, norm_gain, norm_bias):
    vmem = pl.BlockSpec(memory_space=pltpu.VMEM)
    hbm = pl.BlockSpec(memory_space=pl.ANY)
    dma = pltpu.SemaphoreType.DMA
    wide = [high - low for low, high in LANES]
    rows, small = pl.pallas_call(
        kernel,
        out_shape=(
            jax.ShapeDtypeStruct((64, C), F32),
            jax.ShapeDtypeStruct((8, C), F32),
        ),
        in_specs=[hbm, hbm, vmem, vmem, hbm, hbm],
        out_specs=(vmem, vmem),
        scratch_shapes=[
            pltpu.VMEM((3, 3 * C, C), BF16),
            pltpu.VMEM((3 * C, C), BF16),
            pltpu.VMEM((ROWS, COLS, C), BF16),
            pltpu.VMEM((ROWS, COLS, C), BF16),
            pltpu.VMEM((FRAMES, WIDE * ROWS, C), BF16),
            pltpu.VMEM((FRAMES, OWN * ROWS, C), BF16),
            pltpu.VMEM((FRAMES, WIDE * ROWS, C), BF16),
            pltpu.VMEM((FRAMES, OWN * ROWS, C), BF16),
            pltpu.VMEM((FRAMES, 16, C), F32),
            pltpu.VMEM((CELLS_WIDE, 3 * C), BF16),
            pltpu.VMEM((9 * C + 48, CELLS), BF16),
            pltpu.VMEM((8, 384, CELLS), BF16),
            pltpu.VMEM((CELLS, 3 * C), BF16),
            pltpu.VMEM((3 * C + 16, CELLS), BF16),
            pltpu.VMEM((8, 144, CELLS), BF16),
            pltpu.VMEM((2, CELLS, C), BF16),
            pltpu.VMEM((2, CELLS, C), BF16),
            pltpu.VMEM((CELLS_WIDE, C), BF16),
            pltpu.VMEM((TILES, CELLS_WIDE, 128), F32),
            *[pltpu.VMEM((8, 8, BLOCK, n), BF16) for n in wide],
            *[pltpu.VMEM((3, 16, BLOCK, n), BF16) for n in wide],
            *[pltpu.VMEM((16, BLOCK, n), BF16) for n in wide],
            *[pltpu.VMEM((15, BLOCK, n), BF16) for n in wide],
            pltpu.VMEM((16, 8, C), F32),
            pltpu.VMEM((8, 8, C), F32),
            dma((10,)),
            dma((2,)),
            dma((8,)), dma((8,)),
            dma((8,)), dma((8,)),
            dma((8,)), dma((8,)),
            dma((4,)), dma((4,)),
            dma((8,)), dma((8,)),
            dma((UNITS, 3)), dma((UNITS, 3)),
            dma((UNITS,)), dma((UNITS,)),
            dma, dma,
            dma, dma,
        ],
        compiler_params=pltpu.CompilerParams(
            collective_id=0, has_side_effects=True, vmem_limit_bytes=64 * 2**20 - 2**17
        ),
    )(
        clips_in.reshape(ROWS, COLS, C), teacher.reshape(ROWS, COLS, C), norm_gain, norm_bias,
        spatial_weight, temporal_weight.reshape(3 * C, C),
    )
    spatial_grad, temporal_grad, gain_grad, bias_grad, loss = pl.pallas_call(
        finish,
        out_shape=(
            jax.ShapeDtypeStruct((45, C), F32),
            jax.ShapeDtypeStruct((15, C), F32),
            jax.ShapeDtypeStruct((C,), F32),
            jax.ShapeDtypeStruct((C,), F32),
            jax.ShapeDtypeStruct((1, 1), F32),
        ),
        in_specs=[vmem, vmem],
        out_specs=(vmem, vmem, vmem, vmem, pl.BlockSpec(memory_space=pltpu.SMEM)),
    )(rows, small)
    return (spatial_grad, temporal_grad, gain_grad, bias_grad, loss.reshape(()))


def solution(mesh):
    return jax.shard_map(
        shards,
        mesh=mesh,
        in_specs=(
            P("dp", "frame", None, None, None),
            P("dp", "frame", None, None, None),
            P(),
            P(),
            P(),
            P(),
        ),
        out_specs=(P(("dp", "frame"), None), P(("dp", "frame"), None), P(), P(), P()),
        check_vma=False,
    )
```

profile of v0, /device:TPU:1, one launch (start us, length us, event | category | flops | bytes accessed | tf_op | source)
XLA Modules:
  0.0 92.9 jit_solution(17047547432757669309)
XLA Ops:
  0.6 90.7 %shard_map.101 = (f32[64,640]{1,0:T(8,128)}, f32[8,640]{1,0:T(8,128)}) custom-call(bf16[8,96,640]{2,1,0:T(8,128)(2,1)} %bitcast.5, bf16[8,96,640]{2,1,0:T(8,128)(2,1)} %bitcast.6, f32[640]{0:T(1024)} %gain_ref.1, f32[640]{0:T(1024)} %bias_ref.1, bf16[3,3,640,640]{3,2,1,0:T(8,128)(2,1)} %w_hbm.1, bf16[1920,640]{1,0:T(8,128)(2,1)} %bitcast.4), custom_call_target="tpu_custom_call" | custom-call | tf_op jit(solution)/shard_map/pallas_call | solution.py:689
  91.3 1.6 %shard_map.102 = (f32[45,640]{1,0:T(8,128)}, f32[15,640]{1,0:T(8,128)}, f32[640]{0:T(1024)}, f32[640]{0:T(1024)}, f32[1,1]{1,0:T(1,128)}) custom-call(f32[64,640]{1,0:T(8,128)} %get-tuple-element.12.rows, f32[8,640]{1,0:T(8,128)} %get-tuple-element.13.small), custom_call_target="tpu_custom_call" | custom-call | tf_op jit(solution)/shard_map/pallas_call | solution.py:742
where the time goes:
time: 93.1 us; the launch traced here: 92.9 us
  Pallas kernels  92.3 us (99%)
    pallas_call x1, Pallas kernels, shards(): pl.pallas_call(kernel, out_shape=(jax.ShapeDtypeStruct((64, C), F32), jax...  90.7 us

commit v1 on v0

--- a/solution.py
+++ b/solution.py
@@ -58,6 +58,12 @@
         x, y, z = steps
         return (self.dp_x[x] + self.dp_y[y] + self.core, self.fr_z[z] + self.fr_x[x])
 
+    def nth_group(self, n):
+        k = rem(n, 4)
+        step = jnp.where(k == 0, 2, jnp.where(k == 1, 1, jnp.where(k == 2, 3, 0)))
+        half = jnp.where(n < 4, 1 - self.xh, self.xh)
+        return half * 4 + rem(self.y + step, 4)
+
     def along_axis(self, axis, step):
         return self.further(*(step if axis == n else 0 for n in range(3)))
 
@@ -70,7 +76,7 @@
 def kernel(
     x_hbm, t_hbm, gain_ref, bias_ref, w_hbm, wt_hbm,
     rows_out, small_out,
-    w, wt, xraw, traw, xs, ts, xr, tr, stats, hid, hid_t, hid_p, s3, s3_t, s3_p, go, gs, xj, acc,
+    w, wt, wtt, xraw, traw, xs, ts, xr, tr, stats, hid, hid_t, hid_p, s3, s3_t, s3_p, go, gs, xj, acc,
     stage0, stage1, stage2, stage3, stage4, stage5,
     r10, r11, r12, r13, r14, r15,
     p20, p21, p22, p23, p24, p25,
@@ -209,6 +215,10 @@
 
     hid_t[9 * C :, :] = jnp.zeros((48, CELLS), BF16)
     s3_t[3 * C :, :] = jnp.zeros((16, CELLS), BF16)
+
+    w_copies.pop().wait()
+    for t in range(3):
+        wtt[t * C : (t + 1) * C, :] = wt[t * C : (t + 1) * C, :].T
 
     row = lax.broadcasted_iota(jnp.int32, (C, C), 0)
     col = lax.broadcasted_iota(jnp.int32, (C, C), 1)
@@ -335,7 +345,7 @@
                     hid_t[top : top + C, dst] = hid[src, a * C : (a + 1) * C].T
 
         def hidden_send(n, carry):
-            hidden_pair(rem(me.group + 1 + n, 8), rows_of(b)).start()
+            hidden_pair(me.nth_group(n), rows_of(b)).start()
             return carry
 
         lax.fori_loop(0, 8, hidden_send, 0)
@@ -384,10 +394,7 @@
                 loss = loss + jnp.sum((error * error).reshape(FRAMES, 8, C), axis=0)
         src = rows_of(b)
         pair_copy(go.at[0, src], go.at[1, src], 1).start()
-        total = None
-        for t in range(3):
-            part = nt(g3[src, t * C : (t + 1) * C], wt[t * C : (t + 1) * C, :])
-            total = part if total is None else total + part
+        total = jnp.dot(g3[src, :], wtt[...], preferred_element_type=F32)
         for k in range(16):
             at = pl.ds(pl.multiple_of(b * 256 + 16 * k, 16), 16)
             value = total[16 * k : 16 * k + 16]
@@ -468,22 +475,21 @@
                     (mx * 8 + me.dp_y[0] + core, me.fr_z[0] + xl),
                 )
 
-    def time_send(n, carry):
-        m = rem(me.group + 1 + n, 8)
-        send_x(3, m)
-        send_y(4, m)
-        send_z(5, m)
-        return carry
-
-    lax.fori_loop(0, 8, time_send, 0)
+    for step in range(1, 4):
+        there = pl.ds(div(me.dp_x[step], 2), 4), pl.ds(me.fr_x[step] * 4, 4)
+        first_send(3, stage[3].at[there], step, r1[3].at[step - 1], me.along_axis(0, step))
+        for mx in range(2):
+            first_send(
+                4, stage[4].at[mx * 4 + me.at[1][step]], step,
+                r1[4].at[step - 1, pl.ds(mx * 8, 8)], me.along_axis(1, step),
+            )
+        there = pl.ds(0, 8), pl.ds(me.fr_z[step], 2)
+        first_send(5, stage[5].at[there], step, r1[5].at[step - 1], me.along_axis(2, step))
 
     wait_pair(gs.at[1], 3)
 
-    def space_group(n):
-        return rem(me.group + 1 + n, 8)
-
     def space_cut(n):
-        m = space_group(n)
+        m = me.nth_group(n)
         half = rem(n, 2) * 384 + 8 * core
         for q in range(8):
             cut = 45 * q % 8
@@ -495,31 +501,31 @@
             stage[2][m, xl * 4 + zz] = rows[32:48]
 
     def space_send(n):
-        m = space_group(n)
+        m = me.nth_group(n)
         send_z(0, m)
         send_y(1, m)
         send_x(2, m)
 
     def space_dot(n):
-        m = space_group(n)
+        m = me.nth_group(n)
         own = hid_t[pl.ds(pl.multiple_of(720 * m + 352 * core, 16), 384), :]
         both = jnp.concatenate([own, hid_p[m]], axis=1)
         out = jnp.dot(both, gs[...].reshape(2 * CELLS, C), preferred_element_type=F32)
         put(pl.ds(pl.multiple_of(rem(n, 2) * 384, 128), 384), out)
 
-    hidden_pair(space_group(0)).wait_recv()
-    space_dot(0)
+    hidden_pair(me.nth_group(jnp.int32(0))).wait_recv()
+    space_dot(jnp.int32(0))
 
     def space_body(n, carry):
-        hidden_pair(space_group(n)).wait_recv()
+        hidden_pair(me.nth_group(n)).wait_recv()
         space_cut(n - 1)
         space_dot(n)
         space_send(n - 1)
         return carry
 
     lax.fori_loop(1, 8, space_body, 0)
-    space_cut(7)
-    space_send(7)
+    space_cut(jnp.int32(7))
+    space_send(jnp.int32(7))
 
     put(pl.ds(CELLS, 2 * SLAB), jnp.zeros((2 * SLAB, C), F32))
 
@@ -573,9 +579,15 @@
                     q = me.fr_z[step_one] + me.fr_x[step_two]
                     k = me.dp_x[step_two] + q
                     own = stage[u][div(me.dp_x[step_two], 2) + me.y, q]
+                if u == 3:
+                    k = (y, z)
+                elif u == 5:
+                    k = (x_half * 4 + y, xl)
+                else:
+                    k = (k,)
                 total = own.astype(F32)
                 for s in range(3):
-                    total = total + r1[u][s, k].astype(F32)
+                    total = total + r1[u][(s, *k)].astype(F32)
                 p2[u][n] = total.astype(BF16)
                 if n > 0:
                     plane_copy(
@@ -696,6 +708,7 @@
         out_specs=(vmem, vmem),
         scratch_shapes=[
             pltpu.VMEM((3, 3 * C, C), BF16),
+            pltpu.VMEM((3 * C, C), BF16),
             pltpu.VMEM((3 * C, C), BF16),
             pltpu.VMEM((ROWS, COLS, C), BF16),
             pltpu.VMEM((ROWS, COLS, C), BF16),
@@ -715,7 +728,10 @@
             pltpu.VMEM((CELLS_WIDE, C), BF16),
             pltpu.VMEM((TILES, CELLS_WIDE, 128), F32),
             *[pltpu.VMEM((8, 8, BLOCK, n), BF16) for n in wide],
-            *[pltpu.VMEM((3, 16, BLOCK, n), BF16) for n in wide],
+            *[pltpu.VMEM((3, 16, BLOCK, n), BF16) for n in wide[:3]],
+            pltpu.VMEM((3, 4, 4, BLOCK, wide[3]), BF16),
+            pltpu.VMEM((3, 16, BLOCK, wide[4]), BF16),
+            pltpu.VMEM((3, 8, 2, BLOCK, wide[5]), BF16),
             *[pltpu.VMEM((16, BLOCK, n), BF16) for n in wide],
             *[pltpu.VMEM((15, BLOCK, n), BF16) for n in wide],
             pltpu.VMEM((16, 8, C), F32),

time: 93.1 us -> 92.5 us (level)
  no operation moved by 1% of the time
where the time goes in v1:
time: 92.5 us; the launch traced here: 92.4 us
  Pallas kernels  91.7 us (99%)
    pallas_call x1, Pallas kernels, shards(): pl.pallas_call(kernel, out_shape=(jax.ShapeDtypeStruct((64, C), F32), jax...  90.1 us

profile of v1, /device:TPU:1, one launch (start us, length us, event | category | flops | bytes accessed | tf_op | source)
XLA Modules:
  0.0 92.4 jit_solution(8532368943777735842)
XLA Ops:
  0.6 90.1 %shard_map.101 = (f32[64,640]{1,0:T(8,128)}, f32[8,640]{1,0:T(8,128)}) custom-call(bf16[8,96,640]{2,1,0:T(8,128)(2,1)} %bitcast.5, bf16[8,96,640]{2,1,0:T(8,128)(2,1)} %bitcast.6, f32[640]{0:T(1024)} %gain_ref.1, f32[640]{0:T(1024)} %bias_ref.1, bf16[3,3,640,640]{3,2,1,0:T(8,128)(2,1)} %w_hbm.1, bf16[1920,640]{1,0:T(8,128)(2,1)} %bitcast.4), custom_call_target="tpu_custom_call" | custom-call | tf_op jit(solution)/shard_map/pallas_call | solution.py:701
  90.8 1.6 %shard_map.102 = (f32[45,640]{1,0:T(8,128)}, f32[15,640]{1,0:T(8,128)}, f32[640]{0:T(1024)}, f32[640]{0:T(1024)}, f32[1,1]{1,0:T(1,128)}) custom-call(f32[64,640]{1,0:T(8,128)} %get-tuple-element.12.rows, f32[8,640]{1,0:T(8,128)} %get-tuple-element.13.small), custom_call_target="tpu_custom_call" | custom-call | tf_op jit(solution)/shard_map/pallas_call | solution.py:758
